TPU v7x, 32 devices: a whole 2x2x4 slice. The times are simulated.
32 devices in a mesh: space: 16 (over z, y, core), coil: 2 (over x).
Axes of the slice: x: 2, y: 2, z: 4, core: 2. Of those that a mesh axis runs over, the one named last changes fastest.
Arguments:
- spatial_coef: bfloat16 [16, 128, 128, 2, 128], P('coil', 'space'), may hold values from -6 to 6
- temporal_basis: bfloat16 [2, 16, 4], replicated, may hold values from -1.5 to 1.5
- coil_maps: bfloat16 [8, 128, 128, 2, 128], P('coil', 'space'), may hold values from -6 to 6
- field_steps: int32 [128, 128, 128], P('space'), may hold values from 0 to 255
- kspace_data: bfloat16 [8, 4, 128, 128, 2, 128], P('coil', None, None, 'space'), may hold values from -6 to 6
- sample_mask: int32 [4, 128, 128], P(None, 'space'), may hold values 0 or 1
Outputs:
- gradient: float32 [16, 128, 128, 2, 128], P('coil', 'space')
Inputs may be any that keep to these rules, and one draw needn't show every extreme that they name: `sample_mask`: 1 where a phase-encoding line is sampled at that point, else 0.
All inputs are finite; a program needn't handle non-finite values. No bound on the sum of `sample_mask` on one device may be relied on, other than what follows from the above.
Results may differ from a plain program's by a relative error of at most 0.014.
Values may be sent and summed in bfloat16 or wider, within the bound.
No kernel may reach another device: no remote copies, remote signals or barrier semaphores. Data moves between devices by JAX's collectives and lax.ppermute only.
A program may use at most 128 MiB of HBM per device.

v0:
```python
import math

import jax
import jax.numpy as jnp
from jax import lax
from jax.sharding import PartitionSpec as P

STEPS_CYCLE = 256


def dft_table(length, sign):
    index = jnp.arange(length, dtype=jnp.int32)
    steps = index[:, None] * index[None, :] % length
    angle = steps.astype(jnp.float32) * (2.0 * math.pi / length)
    scale = 1.0 / math.sqrt(length)
    cosine = jnp.cos(angle) * scale
    sine = jnp.sin(angle) * (sign * scale)
    upper = jnp.stack([cosine, sine], axis=1)
    lower = jnp.stack([-sine, cosine], axis=1)
    return jnp.stack([upper, lower], axis=0).astype(jnp.bfloat16)


def forward_mix(basis):
    real_part = basis[0]
    imaginary = basis[1]
    return jnp.stack(
        [jnp.stack([real_part, imaginary], -1), jnp.stack([-imaginary, real_part], -1)], 1
    )


def adjoint_mix(basis):
    real_part = basis[0].T
    imaginary = basis[1].T
    return jnp.stack(
        [jnp.stack([real_part, -imaginary], -1), jnp.stack([imaginary, real_part], -1)], 1
    )


def phase_parts(field_steps, points):
    counter = jnp.arange(1, points + 1, dtype=jnp.int32)
    steps = field_steps[None] * counter[:, None, None, None] % STEPS_CYCLE
    angle = steps.astype(jnp.float32) * (2.0 * math.pi / STEPS_CYCLE)
    return (jnp.cos(angle), jnp.sin(angle))


def transform(volume, table, form):
    return jnp.einsum(form, volume, table, preferred_element_type=jnp.float32)


def shards(spatial_coef, temporal_basis, coil_maps, field_steps, kspace_data, sample_mask):
    points = temporal_basis.shape[2]
    section = temporal_basis
    image = jnp.einsum(
        "lxypz,lptq->txyqz",
        lax.all_gather(spatial_coef, "coil", axis=0, tiled=True),
        forward_mix(section),
        preferred_element_type=jnp.float32,
    )
    cosine, sine = phase_parts(field_steps, points)
    image_real = image[:, :, :, 0]
    image_imaginary = image[:, :, :, 1]
    turned_real = cosine * image_real - sine * image_imaginary
    turned_imaginary = sine * image_real + cosine * image_imaginary
    map_real = coil_maps[:, :, :, 0].astype(jnp.float32)[:, None]
    map_imaginary = coil_maps[:, :, :, 1].astype(jnp.float32)[:, None]
    coil_real = map_real * turned_real - map_imaginary * turned_imaginary
    coil_imaginary = map_real * turned_imaginary + map_imaginary * turned_real
    coil_image = jnp.stack([coil_real, coil_imaginary], axis=4).astype(jnp.bfloat16)
    depth_count = coil_image.shape[5]
    row_count = coil_image.shape[3]
    depth_pass = transform(coil_image, dft_table(depth_count, -1.0), "ctxypz,pzqk->ctxyqk").astype(
        jnp.bfloat16
    )
    row_pass = transform(depth_pass, dft_table(row_count, -1.0), "ctxypz,pyqk->ctxkqz").astype(
        jnp.bfloat16
    )
    slabs = lax.all_to_all(row_pass, "space", split_axis=3, concat_axis=2, tiled=True)
    first_count = slabs.shape[2]
    kspace = transform(slabs, dft_table(first_count, -1.0), "ctxypz,pxqk->ctkyqz")
    mask_float = sample_mask.astype(jnp.float32)[None, :, None, :, None, :]
    residual = (mask_float * (kspace - kspace_data.astype(jnp.float32))).astype(jnp.bfloat16)
    back_first = transform(residual, dft_table(first_count, 1.0), "ctxypz,pxqk->ctkyqz").astype(
        jnp.bfloat16
    )
    returned = lax.all_to_all(back_first, "space", split_axis=2, concat_axis=3, tiled=True)
    back_rows = transform(returned, dft_table(row_count, 1.0), "ctxypz,pyqk->ctxkqz").astype(
        jnp.bfloat16
    )
    back_image = transform(back_rows, dft_table(depth_count, 1.0), "ctxypz,pzqk->ctxyqk")
    back_real = back_image[:, :, :, :, 0]
    back_imaginary = back_image[:, :, :, :, 1]
    sum_real = jnp.sum(map_real * back_real + map_imaginary * back_imaginary, axis=0)
    sum_imaginary = jnp.sum(map_real * back_imaginary - map_imaginary * back_real, axis=0)
    combined_real = cosine * sum_real + sine * sum_imaginary
    combined_imaginary = cosine * sum_imaginary - sine * sum_real
    combined = jnp.stack([combined_real, combined_imaginary], axis=3)
    section = temporal_basis.astype(jnp.float32)
    return lax.psum_scatter(
        jnp.einsum(
            "txypz,tplq->lxyqz", combined, adjoint_mix(section), precision=lax.Precision.HIGHEST
        ).astype(jnp.bfloat16),
        "coil",
        scatter_dimension=0,
        tiled=True,
    ).astype(jnp.float32)


def solution(mesh):
    in_specs = (
        P("coil", "space", None, None, None),
        P(),
        P("coil", "space", None, None, None),
        P("space", None, None),
        P("coil", None, None, "space", None, None),
        P(None, "space", None),
    )
    out_specs = P("coil", "space", None, None, None)
    return jax.shard_map(shards, mesh=mesh, in_specs=in_specs, out_specs=out_specs, check_vma=False)
```

profile of v0, /device:TPU:0, one launch (start us, length us, event | category | flops | bytes accessed | tf_op | source)
XLA Modules:
  0.0 778.1 jit_solution(9629277728877845220)
XLA Ops:
  6.5 9.1 %copy.88 = bf16[8,8,128,2,128]{4,0,3,2,1:T(8,128)(2,1)} copy(bf16[8,8,128,2,128]{4,3,2,1,0:T(2,128)(2,1)} %param.6) | data formatting | bytes 8388608 | tf_op args[0]
  17.2 9.5 %slice_convert_fusion.1 = (f32[4,8,128,1,128]{4,3,2,1,0:T(1,128)S(1)}, f32[4,8,128,1,128]{4,3,2,1,0:T(1,128)}) fusion(bf16[4,8,128,2,128]{4,3,2,1,0:T(2,128)(2,1)} %param.8), kind=kLoop, calls=%fused_computation.68 | loop fusion | flops 1048576 | bytes 6291456 | tf_op jit(solution)/shard_map/convert_element_type | solution.py:64
  26.8 95.7 %all-gather.2.cloned.1.call-done = bf16[16,8,128,2,128]{4,0,3,2,1:T(8,128)(2,1)} async-done(((bf16[8,8,128,2,128]{4,0,3,2,1:T(8,128)(2,1)}), bf16[16,8,128,2,128]{4,0,3,2,1:T(8,128)(2,1)}) %all-gather.2.cloned.1.call-update) | async-done | bytes 8388624 | tf_op jit(solution)/shard_map/all_gather | solution.py:55
  122.5 4.7 fusion.32
  128.2 8.7 %multiply_subtract_fusion = (f32[4,8,128,128]{3,2,1,0:T(8,128)S(1)}, f32[4,8,128,128]{3,2,1,0:T(8,128)S(1)}) fusion(f32[4,8,128,2,128]{4,2,1,0,3:T(8,128)S(1)} %bitcast.272, s32[4]{0:T(128)S(1)} %iota_add_fusion, s32[8,128,128]{2,1,0:T(8,128)S(1)} %copy-done.1), kind=kLoop, calls=%fused_computation.67 | loop fusion | flops 10485760 | bytes 8912912 | tf_op jit(solution)/shard_map/sub | solution.py:62
  136.9 4.4 subtract_convert_fusion
  141.3 9.3 %fusion.2 = bf16[4,4,8,128,2,128]{5,3,2,1,0,4:T(8,128)(2,1)} fusion(bf16[4,4,8,128,1,128]{5,3,4,2,1,0:T(8,128)(2,1)} %get-tuple-element.8, bf16[4,4,8,128,1,128]{5,3,4,2,1,0:T(8,128)(2,1)} %get-tuple-element.7, bf16[1,128,2,128]{3,1,0,2:T(8,128)(2,1)S(1)} %get-tuple-element.16, bf16[1,128,2,128]{3,1,0,2:T(8,128)(2,1)S(1)} %get-tuple-element.17), kind=kOutput, calls=%fused_computation.9 | convolution fusion | flops 4320657408 | bytes 16908288 | tf_op jit(solution)/shard_map/ctxypz,pyqk->ctxkqz/dot_general | solution.py:47
  150.7 12.0 %copy.91 = bf16[4,4,8,128,2,128]{5,2,1,0,4,3:T(8,128)(2,1)} copy(bf16[4,4,8,128,2,128]{5,3,2,1,0,4:T(8,128)(2,1)} %fusion.2) | data formatting | bytes 16777216 | tf_op jit(solution)/shard_map/convert_element_type | solution.py:74
  162.7 6.0 all-to-all-start
  168.7 150.7 %all-to-all-done = bf16[4,4,8,128,2,128]{5,2,1,0,4,3:T(8,128)(2,1)} async-done(((bf16[4,4,8,128,2,128]{5,2,1,0,4,3:T(8,128)(2,1)}), bf16[4,4,8,128,2,128]{5,2,1,0,4,3:T(8,128)(2,1)}, u32[]{:S(2)}, u32[]{:S(2)}) %all-to-all-start) | async-done | bytes 8388640 | tf_op jit(solution)/shard_map/all_to_all | solution.py:77
  319.4 16.5 %copy.93 = bf16[4,4,16,8,8,2,128]{6,4,5,3,2,1,0:T(8,128)(2,1)} copy(bf16[4,4,16,8,8,2,128]{6,3,1,0,5,4,2:T(8,128)(2,1)} %bitcast.53) | data formatting | bytes 16777216 | tf_op jit(solution)/shard_map/all_to_all | solution.py:77
  335.8 12.2 %fusion.1 = bf16[4,4,128,8,2,128]{5,2,3,1,0,4:T(8,128)(2,1)S(1)} fusion(bf16[4,4,128,8,2,128]{5,4,3,2,1,0:T(2,128)(2,1)} %param.10, f32[4,8,128]{2,1,0:T(8,128)S(1)} %convert_element_type.142, bf16[4,4,128,8,2,128]{5,3,4,2,1,0:T(8,128)(2,1)} %bitcast.273, bf16[1,128,2,128]{3,1,0,2:T(8,128)(2,1)S(1)} %get-tuple-element.16, ...), kind=kOutput, calls=%fused_computation.3 | convolution fusion | flops 2164523008 | bytes 25313280 | tf_op jit(solution)/shard_map/ctxypz,pxqk->ctkyqz/dot_general | solution.py:47
  348.1 5.8 fusion.3
  353.8 12.0 %copy.99 = bf16[4,4,128,8,2,128]{5,3,1,0,4,2:T(8,128)(2,1)} copy(bf16[4,4,128,8,2,128]{5,2,3,1,0,4:T(8,128)(2,1)} %fusion.3) | data formatting | bytes 16777216 | tf_op jit(solution)/shard_map/convert_element_type | solution.py:82
  365.8 36.5 %all-to-all-start.1 = ((bf16[4,4,128,8,2,128]{5,3,1,0,4,2:T(8,128)(2,1)}), bf16[4,4,128,8,2,128]{5,3,1,0,4,2:T(8,128)(2,1)}, u32[]{:S(2)}, u32[]{:S(2)}) async-start(bf16[4,4,128,8,2,128]{5,3,1,0,4,2:T(8,128)(2,1)} %copy.99), calls=%async_computation.1 | async-start | bytes 16777216 | tf_op jit(solution)/shard_map/all_to_all | solution.py:85
  402.5 150.6 %all-to-all-done.1 = bf16[4,4,128,8,2,128]{5,3,1,0,4,2:T(8,128)(2,1)} async-done(((bf16[4,4,128,8,2,128]{5,3,1,0,4,2:T(8,128)(2,1)}), bf16[4,4,128,8,2,128]{5,3,1,0,4,2:T(8,128)(2,1)}, u32[]{:S(2)}, u32[]{:S(2)}) %all-to-all-start.1) | async-done | bytes 8388640 | tf_op jit(solution)/shard_map/all_to_all | solution.py:85
  553.1 11.0 %convolution_bitcast_fusion = f32[4,4,8,128,2,128]{5,3,4,2,1,0:T(8,128)} fusion(bf16[4,4,8,16,8,2,128]{6,4,1,0,5,2,3:T(8,128)(2,1)} %bitcast.65, bf16[1,128,2,128]{3,1,2,0:T(8,128)(2,1)S(1)} %get-tuple-element.18, bf16[1,128,2,128]{3,1,2,0:T(8,128)(2,1)S(1)} %get-tuple-element.15), kind=kOutput, calls=%fused_computation.8 | convolution fusion | flops 4299685888 | bytes 25296896 | tf_op jit(solution)/shard_map/ctxypz,pzqk->ctxyqk/dot_general | solution.py:47
  564.1 8.2 %add_reduce_fusion = (f32[4,8,128,128]{3,2,1,0:T(8,128)S(1)}, f32[4,8,128,128]{3,2,1,0:T(8,128)S(1)}) fusion(f32[4,4,8,128,2,128]{5,3,4,2,1,0:T(8,128)} %convolution_bitcast_fusion, f32[4,8,128,128]{3,2,1,0:T(8,128)} %bitcast.269, f32[4,8,128,128]{3,2,1,0:T(8,128)S(1)} %bitcast.268), kind=kLoop, calls=%fused_computation.32 | loop fusion | flops 15728640 | bytes 25165824 | tf_op jit(solution)/shard_map/reduce_sum | solution.py:92
  572.3 18.5 %fusion.41 = (f32[4,8,128,1,128]{4,0,3,2,1:T(4,128)S(1)}, f32[4,8,128,1,128]{4,0,3,2,1:T(4,128)S(1)}) fusion(f32[4,8,128,128]{3,2,1,0:T(8,128)S(1)} %get-tuple-element.6, f32[4,8,128,128]{3,2,1,0:T(8,128)S(1)} %get-tuple-element.5, s32[4]{0:T(128)S(1)} %iota_add_fusion, s32[8,128,128]{2,1,0:T(8,128)S(1)} %copy-done.1), kind=kLoop, calls=%fused_computation.61 | loop fusion | flops 10485760 | bytes 8912912 | tf_op jit(solution)/shard_map/add | solution.py:94
  590.8 17.0 %fusion.4 = bf16[16,8,128,2,128]{4,0,2,1,3:T(8,128)(2,1)} fusion(f32[4,8,128,1,128]{4,0,3,2,1:T(4,128)S(1)} %get-tuple-element.10, f32[4,8,128,1,128]{4,0,3,2,1:T(4,128)S(1)} %get-tuple-element.9, f32[4,2,16,2,1,1]{2,0,1,5,4,3:T(4,128)S(1)} %maximum_bitcast_fusion.27), kind=kOutput, calls=%fused_computation.11 | convolution fusion | flops 407896064 | bytes 12583936 | tf_op jit(solution)/shard_map/txypz,tplq->lxyqz/dot_general | solution.py:99
  607.8 8.9 %copy.139 = bf16[16,8,128,2,128]{4,2,1,3,0:T(8,128)(2,1)} copy(bf16[16,8,128,2,128]{4,0,2,1,3:T(8,128)(2,1)} %fusion.4) | data formatting | bytes 16777216
  616.6 10.3 %copy.174 = bf16[2,8,2048,128]{3,1,2,0:T(8,128)(2,1)} copy(bf16[2,8,2048,128]{3,2,1,0:T(8,128)(2,1)} %bitcast.266) | data formatting | bytes 16777216
  627.0 130.3 %reduce-scatter.4.cloned.1.call-done = bf16[8,262144]{1,0:T(8,128)(2,1)} async-done(((bf16[16,262144]{1,0:T(8,128)(2,1)}), bf16[8,262144]{1,0:T(8,128)(2,1)}) %reduce-scatter.4.cloned.1.call-update) | async-done | bytes 4194320
  763.5 7.6 copy.107
  (29 shorter events, 8.8 us)
Async XLA Ops:
  6.5 116.0 %all-gather.2.cloned.1.call-start = ((), (), s32[]{:S(2)}) async-start(), calls=%async_computation.3 | async-start | bytes 12582912 | tf_op jit(solution)/shard_map/all_gather | solution.py:55
  15.7 0.7 copy-start.3
  127.2 1.0 copy-start.1
  128.2 8.7 %copy-start = (f32[4,8,128,1,128]{4,3,2,1,0:T(1,128)S(1)}, f32[4,8,128,1,128]{4,3,2,1,0:T(1,128)}, u32[]{:S(2)}) copy-start(f32[4,8,128,1,128]{4,3,2,1,0:T(1,128)} %get-tuple-element.14) | copy-start | bytes 6291460
  162.7 6.0 copy-start.2
  162.7 156.7 %all-to-all-start = ((bf16[4,4,8,128,2,128]{5,2,1,0,4,3:T(8,128)(2,1)}), bf16[4,4,8,128,2,128]{5,2,1,0,4,3:T(8,128)(2,1)}, u32[]{:S(2)}, u32[]{:S(2)}) async-start(bf16[4,4,8,128,2,128]{5,2,1,0,4,3:T(8,128)(2,1)} %copy.91), calls=%async_computation | async-start | bytes 16777216 | tf_op jit(solution)/shard_map/all_to_all | solution.py:77
  365.8 187.3 %all-to-all-start.1 = ((bf16[4,4,128,8,2,128]{5,3,1,0,4,2:T(8,128)(2,1)}), bf16[4,4,128,8,2,128]{5,3,1,0,4,2:T(8,128)(2,1)}, u32[]{:S(2)}, u32[]{:S(2)}) async-start(bf16[4,4,128,8,2,128]{5,3,1,0,4,2:T(8,128)(2,1)} %copy.99), calls=%async_computation.1 | async-start | bytes 16777216 | tf_op jit(solution)/shard_map/all_to_all | solution.py:85
  402.4 354.9 %reduce-scatter.4.cloned.1.call-start = ((), (), s32[]{:S(2)}) async-start(), calls=%async_computation.4 | async-start | bytes 12582912
Sparse Core Ops, SparseCore 0:
  15.8 106.6 all-gather.1
  627.1 130.1 reduce-scatter.3
where the time goes:
time: 787 us; the launch traced here: 778 us
  waiting for transfers between devices  527 us (67%)
  local copies, waits for them, and re-layouts  80.9 us (10%)
  matrix products  59.9 us (8%)
  other arithmetic  53.7 us (7%)
  starting transfers between devices  42.6 us (5%)
  between operations  13.8 us (2%)
    all_to_all x1, waiting for transfers between devices, shards(): lax.all_to_all(row_pass, 'space', split_axis=3, concat_axis=2, tiled=True)  151 us
    all_to_all x1, waiting for transfers between devices, shards(): lax.all_to_all(back_first, 'space', split_axis=2, concat_axis=3, tiled=True)  151 us
    unnamed x3, waiting for transfers between devices  130 us
    all_gather x1, waiting for transfers between devices, shards(): lax.all_gather(spatial_coef, 'coil', axis=0, tiled=True)  95.7 us
    dot_general x4, matrix products, transform(): return jnp.einsum(form, volume, table, preferred_element_type=jnp.float32)  38.3 us
    all_to_all x1, starting transfers between devices, shards(): lax.all_to_all(back_first, 'space', split_axis=2, concat_axis=3, tiled=True)  36.5 us
    unnamed x12, local copies, waits for them, and re-layouts  31.7 us
    add x1, other arithmetic, shards(): combined_real = cosine * sum_real + sine * sum_imaginary  18.5 us
  transfers between devices with their start and end apart: 4, of which 4 were waited for; matrix products, arithmetic and copies ran while one was open for 1% of the time, Pallas kernels for 0%

commit v1 on v0

v1 whole, which is shorter than its diff:
```python
import math

import jax
import jax.numpy as jnp
from jax import lax
from jax.sharding import PartitionSpec as P

STEPS_CYCLE = 256


def dft_table(length, sign):
    index = jnp.arange(length, dtype=jnp.int32)
    steps = index[:, None] * index[None, :] % length
    angle = steps.astype(jnp.float32) * (2.0 * math.pi / length)
    scale = 1.0 / math.sqrt(length)
    cosine = jnp.cos(angle) * scale
    sine = jnp.sin(angle) * (sign * scale)
    upper = jnp.stack([cosine, sine], axis=1)
    lower = jnp.stack([-sine, cosine], axis=1)
    return jnp.stack([upper, lower], axis=0).astype(jnp.bfloat16)


def forward_mix(basis):
    real_part = basis[0]
    imaginary = basis[1]
    return jnp.stack(
        [jnp.stack([real_part, imaginary], -1), jnp.stack([-imaginary, real_part], -1)], 1
    )


def adjoint_mix(basis):
    real_part = basis[0].T
    imaginary = basis[1].T
    return jnp.stack(
        [jnp.stack([real_part, -imaginary], -1), jnp.stack([imaginary, real_part], -1)], 1
    )


def phase_parts(field_steps, points):
    counter = jnp.arange(1, points + 1, dtype=jnp.int32)
    steps = field_steps[None] * counter[:, None, None, None] % STEPS_CYCLE
    angle = steps.astype(jnp.float32) * (2.0 * math.pi / STEPS_CYCLE)
    return (jnp.cos(angle), jnp.sin(angle))


def transform(volume, table, form):
    return jnp.einsum(form, volume, table, preferred_element_type=jnp.float32)


def over_groups(part, axis):
    groups = lax.axis_size(axis)
    sent = part.astype(jnp.bfloat16)
    total = part
    for shift in range(1, groups):
        pairs = [(g, (g + shift) % groups) for g in range(groups)]
        total = total + lax.ppermute(sent, axis, pairs).astype(jnp.float32)
    return total


def shards(spatial_coef, temporal_basis, coil_maps, field_steps, kspace_data, sample_mask):
    points = temporal_basis.shape[2]
    ranks = spatial_coef.shape[0]
    basis = lax.dynamic_slice_in_dim(
        temporal_basis, lax.axis_index("coil") * ranks, ranks, axis=1
    )
    first_count = kspace_data.shape[2]
    row_count = coil_maps.shape[2]
    depth_count = coil_maps.shape[4]
    mask_here = sample_mask.astype(jnp.bfloat16)
    mask_all = lax.all_gather(mask_here, "space", axis=1, tiled=True)
    arrived = []
    for t in range(points):
        measured = kspace_data[:, t] * mask_here[t][None, None, :, None, :]
        local = transform(measured, dft_table(first_count, 1.0), "cxypz,pxqk->ckyqz").astype(
            jnp.bfloat16
        )
        arrived.append(lax.all_to_all(local, "space", split_axis=1, concat_axis=2, tiled=True))
    cosine, sine = phase_parts(field_steps, points)
    map_real = coil_maps[:, :, :, 0].astype(jnp.float32)
    map_imaginary = coil_maps[:, :, :, 1].astype(jnp.float32)
    mixed = forward_mix(basis)
    combined = []
    for t in range(points):
        image = over_groups(
            jnp.einsum(
                "lxypz,lpq->xyqz",
                spatial_coef,
                mixed[:, :, t],
                preferred_element_type=jnp.float32,
            ),
            "coil",
        )
        turned_real = cosine[t] * image[:, :, 0] - sine[t] * image[:, :, 1]
        turned_imaginary = sine[t] * image[:, :, 0] + cosine[t] * image[:, :, 1]
        coil_real = map_real * turned_real - map_imaginary * turned_imaginary
        coil_imaginary = map_real * turned_imaginary + map_imaginary * turned_real
        coil_image = jnp.stack([coil_real, coil_imaginary], axis=3).astype(jnp.bfloat16)
        depth_pass = transform(coil_image, dft_table(depth_count, -1.0), "cxypz,pzqk->cxyqk")
        row_pass = transform(
            depth_pass.astype(jnp.bfloat16), dft_table(row_count, -1.0), "cxypz,pyqk->cxkqz"
        )
        mask_float = mask_all[t].astype(jnp.float32)[None, None, :, None, :]
        back_first = (mask_float * row_pass - arrived[t].astype(jnp.float32)).astype(jnp.bfloat16)
        back_rows = transform(back_first, dft_table(row_count, 1.0), "cxypz,pyqk->cxkqz")
        back_image = transform(
            back_rows.astype(jnp.bfloat16), dft_table(depth_count, 1.0), "cxypz,pzqk->cxyqk"
        )
        back_real = back_image[:, :, :, 0]
        back_imaginary = back_image[:, :, :, 1]
        sum_real = jnp.sum(map_real * back_real + map_imaginary * back_imaginary, axis=0)
        sum_imaginary = jnp.sum(map_real * back_imaginary - map_imaginary * back_real, axis=0)
        combined_real = cosine[t] * sum_real + sine[t] * sum_imaginary
        combined_imaginary = cosine[t] * sum_imaginary - sine[t] * sum_real
        combined.append(
            over_groups(jnp.stack([combined_real, combined_imaginary], axis=2), "coil")
        )
    return jnp.einsum(
        "txypz,tplq->lxyqz",
        jnp.stack(combined),
        adjoint_mix(basis.astype(jnp.float32)),
        precision=lax.Precision.HIGHEST,
    )


def solution(mesh):
    in_specs = (
        P("coil", "space", None, None, None),
        P(),
        P("coil", "space", None, None, None),
        P("space", None, None),
        P("coil", None, None, "space", None, None),
        P(None, "space", None),
    )
    out_specs = P("coil", "space", None, None, None)
    return jax.shard_map(shards, mesh=mesh, in_specs=in_specs, out_specs=out_specs, check_vma=False)
```

time: 787 us -> 345 us (0.44)
  waiting for transfers between devices: 527 us -> 94.6 us
  local copies, waits for them, and re-layouts: 80.9 us -> 43.2 us
  blocking collectives: 0 us -> 35.7 us
  between operations: 13.8 us -> 0.66 us
  matrix products: 59.9 us -> 72 us
  other arithmetic: 53.7 us -> 42.3 us
    all_to_all x2 -> x4, waiting for transfers between devices: 301 us -> 51.6 us  [shards(): lax.all_to_all(local, 'space', split_axis=1, concat_axis=2, tiled=True)]
    unnamed x3 -> x0, waiting for transfers between devices: 130 us -> none
    all_gather x1 -> x0, waiting for transfers between devices: 95.7 us -> none  [shards(): lax.all_gather(spatial_coef, 'coil', axis=0, tiled=True)]
    ppermute x0 -> x8, waiting for transfers between devices: none -> 43 us  [over_groups(): total = total + lax.ppermute(sent, axis, pairs).astype(jnp.float32)]
    all_gather x0 -> x1, blocking collectives: none -> 35.7 us  [shards(): mask_all = lax.all_gather(mask_here, 'space', axis=1, tiled=True)]
    unnamed x12 -> x50, local copies, waits for them, and re-layouts: 31.7 us -> 4.2 us
    convert_element_type x3 -> x4, local copies, waits for them, and re-layouts: 31.7 us -> 10.8 us  [shards(): transform(measured, dft_table(first_count, 1.0), 'cxypz,pxqk->ckyqz')]
    mul x0 -> x3, other arithmetic: none -> 13.4 us  [the longest x1 10.2 us: shards(): measured = kspace_data[:, t] * mask_here[t][None, None, :, None, :]]
  transfers between devices with their start and end apart: 4 -> 12, of which waited for: 4 -> 6; matrix products, arithmetic and copies ran while one was open for 1% -> 31% of each run, Pallas kernels for 0% -> 0%
where the time goes in v1:
time: 345 us; the launch traced here: 338 us
  waiting for transfers between devices  94.6 us (27%)
  matrix products  72 us (21%)
  starting transfers between devices  49.8 us (14%)
  local copies, waits for them, and re-layouts  43.2 us (13%)
  other arithmetic  42.3 us (12%)
  blocking collectives  35.7 us (10%)
    all_to_all x4, waiting for transfers between devices, shards(): lax.all_to_all(local, 'space', split_axis=1, concat_axis=2, tiled=True)  51.6 us
    dot_general x16, matrix products, transform(): return jnp.einsum(form, volume, table, preferred_element_type=jnp.float32)  49 us
    ppermute x8, waiting for transfers between devices, over_groups(): total = total + lax.ppermute(sent, axis, pairs).astype(jnp.float32)  43 us
    all_to_all x4, starting transfers between devices, shards(): lax.all_to_all(local, 'space', split_axis=1, concat_axis=2, tiled=True)  41.5 us
    all_gather x1, blocking collectives, shards(): mask_all = lax.all_gather(mask_here, 'space', axis=1, tiled=True)  35.7 us
    dot_general x4, matrix products, shards(): jnp.einsum('lxypz,lpq->xyqz', spatial_coef, mixed[:, :, t], preferred_ele...  13.7 us
    all_to_all x4, local copies, waits for them, and re-layouts, shards(): lax.all_to_all(local, 'space', split_axis=1, concat_axis=2, tiled=True)  11.6 us
    convert_element_type x4, local copies, waits for them, and re-layouts, shards(): transform(measured, dft_table(first_count, 1.0), 'cxypz,pxqk->ckyqz')  10.8 us
  transfers between devices with their start and end apart: 12, of which 6 were waited for; matrix products, arithmetic and copies ran while one was open for 31% of the time, Pallas kernels for 0%

profile of v1, /device:TPU:0, one launch (start us, length us, event | category | flops | bytes accessed | tf_op | source)
XLA Modules:
  0.0 338.3 jit_solution(4507583769659401000)
XLA Ops:
  1.6 10.2 %bitcast_multiply_fusion.4 = (bf16[4,128,8,2,128]{4,3,2,1,0:T(2,128)(2,1)}, bf16[4,128,8,2,128]{4,3,2,1,0:T(2,128)(2,1)}, bf16[4,128,8,2,128]{4,3,2,1,0:T(2,128)(2,1)}, bf16[4,128,8,2,128]{4,3,2,1,0:T(2,128)(2,1)S(1)}) fusion(bf16[4,4,128,8,2,128]{5,4,3,2,1,0:T(2,128)(2,1)} %param.10, bf16[8,128]{1,0:T(8,128)(2,1)S(1)} %get-tuple-element.77, ...), kind=kLoop, calls=%fused_computation.142 | loop fusion | flops 4194304 | bytes 16785408 | tf_op jit(solution)/shard_map/mul | solution.py:73
  15.4 7.4 %all-to-all-start.2 = ((bf16[4,128,8,2,128]{4,2,0,3,1:T(8,128)(2,1)}), bf16[4,128,8,2,128]{4,2,0,3,1:T(8,128)(2,1)S(1)}, u32[]{:S(2)}, u32[]{:S(2)}) async-start(bf16[4,128,8,2,128]{4,2,0,3,1:T(8,128)(2,1)} %copy.126), calls=%async_computation.2 | async-start | bytes 4194304 | tf_op jit(solution)/shard_map/all_to_all | solution.py:77
  28.1 35.9 %all-to-all-done.2 = bf16[4,128,8,2,128]{4,2,0,3,1:T(8,128)(2,1)S(1)} async-done(((bf16[4,128,8,2,128]{4,2,0,3,1:T(8,128)(2,1)}), bf16[4,128,8,2,128]{4,2,0,3,1:T(8,128)(2,1)S(1)}, u32[]{:S(2)}, u32[]{:S(2)}) %all-to-all-start.2) | async-done | bytes 2097184 | tf_op jit(solution)/shard_map/all_to_all | solution.py:77
  65.3 11.4 %all-to-all-start.3 = ((bf16[4,128,8,2,128]{4,2,0,3,1:T(8,128)(2,1)}), bf16[4,128,8,2,128]{4,2,0,3,1:T(8,128)(2,1)}, u32[]{:S(2)}, u32[]{:S(2)}) async-start(bf16[4,128,8,2,128]{4,2,0,3,1:T(8,128)(2,1)} %copy.136), calls=%async_computation.3 | async-start | bytes 4194304 | tf_op jit(solution)/shard_map/all_to_all | solution.py:77
  76.9 6.2 %fusion.176 = (bf16[8,128,2,128]{3,2,1,0:T(2,128)(2,1)}, f32[8,128,2,128]{3,2,1,0:T(2,128)}) fusion(bf16[8,8,128,2,128]{4,3,2,1,0:T(2,128)(2,1)} %param.6, bf16[8,2,1,2]{0,2,3,1:T(2,128)(2,1)S(1)} %get-tuple-element.84), kind=kOutput, calls=%fused_computation.302 | convolution fusion | flops 8650752 | bytes 5767232 | tf_op jit(solution)/shard_map/lxypz,lpq->xyqz/dot_general | solution.py:85
  102.0 15.7 %all-to-all-done.3 = bf16[4,128,8,2,128]{4,2,0,3,1:T(8,128)(2,1)} async-done(((bf16[4,128,8,2,128]{4,2,0,3,1:T(8,128)(2,1)}), bf16[4,128,8,2,128]{4,2,0,3,1:T(8,128)(2,1)}, u32[]{:S(2)}, u32[]{:S(2)}) %all-to-all-start.3) | async-done | bytes 2097184 | tf_op jit(solution)/shard_map/all_to_all | solution.py:77
  117.7 11.3 %all-to-all-start.1 = ((bf16[4,128,8,2,128]{4,2,0,3,1:T(8,128)(2,1)}), bf16[4,128,8,2,128]{4,2,0,3,1:T(8,128)(2,1)}, u32[]{:S(2)}, u32[]{:S(2)}) async-start(bf16[4,128,8,2,128]{4,2,0,3,1:T(8,128)(2,1)} %copy.116), calls=%async_computation.1 | async-start | bytes 4194304 | tf_op jit(solution)/shard_map/all_to_all | solution.py:77
  129.0 9.4 %fusion.122 = (f32[4,8,128,128]{3,2,1,0:T(8,128)S(1)}, f32[4,8,128,128]{3,2,1,0:T(8,128)S(1)}) fusion(s32[4]{0:T(128)S(1)} %iota_add_fusion, s32[8,128,128]{2,1,0:T(8,128)} %param.9), kind=kLoop, calls=%fused_computation.177 | loop fusion | flops 7340032 | bytes 4718608 | tf_op jit(solution)/shard_map/cos | solution.py:43
  138.4 4.9 %fusion.174 = (bf16[4,8,128,1,128]{4,3,2,1,0:T(2,128)(2,1)}, bf16[4,8,128,1,128]{4,3,2,1,0:T(2,128)(2,1)}) fusion(bf16[4,8,128,2,128]{4,3,2,1,0:T(2,128)(2,1)S(1)} %copy-done.11), kind=kLoop, calls=%fused_computation.300 | loop fusion | bytes 4194304 | tf_op jit(solution)/shard_map/slice | solution.py:79
  144.3 35.7 %all_gather.3 = bf16[4,128,128]{2,1,0:T(8,128)(2,1)S(1)} all-gather(bf16[4,8,128]{2,1,0:T(8,128)(2,1)S(1)} %convert_element_type.328), channel_id=1, replica_groups=mesh['space'=16,'coil'=2] {'space'}, dimensions={1}, use_global_device_ids=true | all-gather | bytes 139264 | tf_op jit(solution)/shard_map/all_gather | solution.py:70
  191.8 11.4 %all-to-all-start = ((bf16[4,128,8,2,128]{4,2,0,3,1:T(8,128)(2,1)}), bf16[4,128,8,2,128]{4,2,0,3,1:T(8,128)(2,1)}, u32[]{:S(2)}, u32[]{:S(2)}) async-start(bf16[4,128,8,2,128]{4,2,0,3,1:T(8,128)(2,1)} %copy.106), calls=%async_computation | async-start | bytes 4194304 | tf_op jit(solution)/shard_map/all_to_all | solution.py:77
  227.4 4.9 %bitcast_convert_fusion.1 = bf16[2,128,4,8,128]{4,1,0,3,2:T(8,128)(2,1)} fusion(bf16[4,8,128,2,128]{4,2,3,1,0:T(8,128)(2,1)} %bitcast_convert_fusion.7, f32[128,128]{1,0:T(8,128)} %get-tuple-element.70, bf16[1,128,2,128]{3,1,0,2:T(8,128)(2,1)S(1)} %get-tuple-element.74, bf16[1,128,2,128]{3,1,0,2:T(8,128)(2,1)S(1)} %get-tuple-element.73, ...), kind=kOutput, calls=%fused_computation.33 | convolution fusion | flops 1079508992 | bytes 6619136 | tf_op jit(solution)/shard_map/cxypz,pyqk->cxkqz/dot_general | solution.py:47
  236.6 4.9 %bitcast_convert_fusion = bf16[2,128,4,8,128]{4,1,0,3,2:T(8,128)(2,1)} fusion(bf16[4,8,128,2,128]{4,2,3,1,0:T(8,128)(2,1)} %bitcast_convert_fusion.5, f32[128,128]{1,0:T(8,128)} %get-tuple-element.69, bf16[1,128,2,128]{3,1,0,2:T(8,128)(2,1)S(1)} %get-tuple-element.74, bf16[1,128,2,128]{3,1,0,2:T(8,128)(2,1)S(1)} %get-tuple-element.73, ...), kind=kOutput, calls=%fused_computation.32 | convolution fusion | flops 1079508992 | bytes 6619136 | tf_op jit(solution)/shard_map/cxypz,pyqk->cxkqz/dot_general | solution.py:47
  241.5 4.3 %convolution_bitcast_fusion = f32[4,8,128,2,128]{4,2,3,1,0:T(8,128)} fusion(bf16[2,128,4,8,128]{4,1,0,3,2:T(8,128)(2,1)} %bitcast_convert_fusion, bf16[1,128,2,128]{3,1,2,0:T(8,128)(2,1)S(1)} %get-tuple-element.75, bf16[1,128,2,128]{3,1,2,0:T(8,128)(2,1)S(1)} %get-tuple-element.76), kind=kOutput, calls=%fused_computation.78 | convolution fusion | flops 537133056 | bytes 6422528 | tf_op jit(solution)/shard_map/cxypz,pzqk->cxyqk/dot_general | solution.py:47
  245.9 4.8 %bitcast_convert_fusion.2 = bf16[2,128,4,8,128]{4,1,0,3,2:T(8,128)(2,1)} fusion(bf16[4,8,128,2,128]{4,2,3,1,0:T(8,128)(2,1)} %bitcast_convert_fusion.9, f32[128,128]{1,0:T(8,128)S(1)} %get-tuple-element.71, bf16[1,128,2,128]{3,1,0,2:T(8,128)(2,1)S(1)} %get-tuple-element.74, bf16[1,128,2,128]{3,1,0,2:T(8,128)(2,1)S(1)} %get-tuple-element.73, ...), kind=kOutput, calls=%fused_computation.34 | convolution fusion | flops 1079508992 | bytes 6619136 | tf_op jit(solution)/shard_map/cxypz,pyqk->cxkqz/dot_general | solution.py:47
  250.7 4.3 %convolution_bitcast_fusion.2 = f32[4,8,128,2,128]{4,2,3,1,0:T(8,128)} fusion(bf16[2,128,4,8,128]{4,1,0,3,2:T(8,128)(2,1)} %bitcast_convert_fusion.2, bf16[1,128,2,128]{3,1,2,0:T(8,128)(2,1)S(1)} %get-tuple-element.75, bf16[1,128,2,128]{3,1,2,0:T(8,128)(2,1)S(1)} %get-tuple-element.76), kind=kOutput, calls=%fused_computation.80 | convolution fusion | flops 537133056 | bytes 6422528 | tf_op jit(solution)/shard_map/cxypz,pzqk->cxyqk/dot_general | solution.py:47
  258.3 4.8 %bitcast_convert_fusion.3 = bf16[2,128,4,8,128]{4,1,0,3,2:T(8,128)(2,1)} fusion(bf16[4,8,128,2,128]{4,2,3,1,0:T(8,128)(2,1)} %bitcast_convert_fusion.11, f32[128,128]{1,0:T(8,128)S(1)} %get-tuple-element.72, bf16[1,128,2,128]{3,1,0,2:T(8,128)(2,1)S(1)} %get-tuple-element.74, bf16[1,128,2,128]{3,1,0,2:T(8,128)(2,1)S(1)} %get-tuple-element.73, ...), kind=kOutput, calls=%fused_computation.35 | convolution fusion | flops 1079508992 | bytes 6619136 | tf_op jit(solution)/shard_map/cxypz,pyqk->cxkqz/dot_general | solution.py:47
  266.3 5.7 %fusion.26 = (f32[8,128,128]{2,1,0:T(8,128)S(1)}, f32[8,128,128]{2,1,0:T(8,128)S(1)}, f32[8,128,128]{2,1,0:T(8,128)S(1)}, f32[8,128,128]{2,1,0:T(8,128)S(1)}, f3...) fusion(bf16[4,8,128,1,128]{4,2,3,1,0:T(8,128)(2,1)S(1)} %copy-d, ...), kind=kLoop, calls=%fused_computation.90 | loop fusion | flops 16777216 | bytes 23068672 | tf_op jit(solution)/shard_map/reduce_sum | solution.py:110
  277.4 10.1 %collective-permute-done.1 = bf16[8,128,2,128]{3,1,0,2:T(8,128)(2,1)S(1)} collective-permute-done((bf16[8,128,2,128]{3,1,0,2:T(8,128)(2,1)S(1)}, bf16[8,128,2,128]{3,1,0,2:T(8,128)(2,1)S(1)}, u32[]{:S(2)}, u32[]{:S(2)}) %collective-permute-start.1) | collective-permute-done | bytes 524320 | tf_op jit(solution)/shard_map/ppermute | solution.py:56
  287.6 11.1 %collective-permute-done.3 = bf16[8,128,2,128]{3,1,0,2:T(8,128)(2,1)S(1)} collective-permute-done((bf16[8,128,2,128]{3,1,0,2:T(8,128)(2,1)S(1)}, bf16[8,128,2,128]{3,1,0,2:T(8,128)(2,1)S(1)}, u32[]{:S(2)}, u32[]{:S(2)}) %collective-permute-start.3) | collective-permute-done | bytes 524320 | tf_op jit(solution)/shard_map/ppermute | solution.py:56
  298.9 11.1 %collective-permute-done.5 = bf16[8,128,2,128]{3,1,0,2:T(8,128)(2,1)S(1)} collective-permute-done((bf16[8,128,2,128]{3,1,0,2:T(8,128)(2,1)S(1)}, bf16[8,128,2,128]{3,1,0,2:T(8,128)(2,1)S(1)}, u32[]{:S(2)}, u32[]{:S(2)}) %collective-permute-start.5) | collective-permute-done | bytes 524320 | tf_op jit(solution)/shard_map/ppermute | solution.py:56
  310.1 10.6 %collective-permute-done.7 = bf16[8,128,2,128]{3,1,0,2:T(8,128)(2,1)S(1)} collective-permute-done((bf16[8,128,2,128]{3,1,0,2:T(8,128)(2,1)S(1)}, bf16[8,128,2,128]{3,1,0,2:T(8,128)(2,1)S(1)}, u32[]{:S(2)}, u32[]{:S(2)}) %collective-permute-start.7) | collective-permute-done | bytes 524320 | tf_op jit(solution)/shard_map/ppermute | solution.py:56
  321.1 9.3 %fusion.7 = f32[8,8,128,2,128]{4,0,2,1,3:T(8,128)S(1)} fusion(f32[4,8,128,2,128]{4,2,1,3,0:T(8,128)S(1)} %pad_maximum_fusion, f32[4,2,8,2,1,1]{2,0,1,5,4,3:T(4,128)S(1)} %maximum_bitcast_fusion.46), kind=kOutput, calls=%fused_computation.67 | convolution fusion | flops 201326592 | bytes 12583424 | tf_op jit(solution)/shard_map/txypz,tplq->lxyqz/dot_general | solution.py:117
  330.4 7.6 %copy.142 = f32[8,8,128,2,128]{4,3,2,1,0:T(2,128)} copy(f32[8,8,128,2,128]{4,0,2,1,3:T(8,128)S(1)} %fusion.7) | data formatting | bytes 16777216 | tf_op jit(solution)/shard_map/txypz,tplq->lxyqz/transpose | solution.py:117
  (125 shorter events, 84.6 us)
Async XLA Ops:
  15.4 48.5 %all-to-all-start.2 = ((bf16[4,128,8,2,128]{4,2,0,3,1:T(8,128)(2,1)}), bf16[4,128,8,2,128]{4,2,0,3,1:T(8,128)(2,1)S(1)}, u32[]{:S(2)}, u32[]{:S(2)}) async-start(bf16[4,128,8,2,128]{4,2,0,3,1:T(8,128)(2,1)} %copy.126), calls=%async_computation.2 | async-start | bytes 4194304 | tf_op jit(solution)/shard_map/all_to_all | solution.py:77
  28.1 48.6 %copy-start.24 = (bf16[2,16,4]{1,2,0:T(4,128)(2,1)S(1)}, bf16[2,16,4]{1,2,0:T(4,128)(2,1)}, u32[]{:S(2)}) copy-start(bf16[2,16,4]{1,2,0:T(4,128)(2,1)} %param.7) | copy-start | bytes 772
  65.3 52.4 %all-to-all-start.3 = ((bf16[4,128,8,2,128]{4,2,0,3,1:T(8,128)(2,1)}), bf16[4,128,8,2,128]{4,2,0,3,1:T(8,128)(2,1)}, u32[]{:S(2)}, u32[]{:S(2)}) async-start(bf16[4,128,8,2,128]{4,2,0,3,1:T(8,128)(2,1)} %copy.136), calls=%async_computation.3 | async-start | bytes 4194304 | tf_op jit(solution)/shard_map/all_to_all | solution.py:77
  76.9 7.7 %copy-start = (bf16[8,8,128,2,128]{4,3,2,1,0:T(2,128)(2,1)S(1)}, bf16[8,8,128,2,128]{4,3,2,1,0:T(2,128)(2,1)}, u32[]{:S(2)}) copy-start(bf16[8,8,128,2,128]{4,3,2,1,0:T(2,128)(2,1)} %param.6) | copy-start | bytes 12582916
  83.1 100.2 %collective-permute-start = (bf16[8,128,2,128]{3,2,1,0:T(2,128)(2,1)}, bf16[8,128,2,128]{3,2,1,0:T(2,128)(2,1)}, u32[]{:S(2)}, u32[]{:S(2)}) collective-permute-start(bf16[8,128,2,128]{3,2,1,0:T(2,128)(2,1)} %get-tuple-element.91), channel_id=1, source_target_pairs={{0,1},{1,0},{2,3},{3,2},{4,5},{5,4},{6,7},{7,6},{8,9},{9,8},{10,11... | collective-permute-start | bytes 1572872 | tf_op jit(solution)/shard_map/ppermute | solution.py:56
  88.1 97.5 %collective-permute-start.2 = (bf16[8,128,2,128]{3,1,0,2:T(8,128)(2,1)}, bf16[8,128,2,128]{3,1,0,2:T(8,128)(2,1)}, u32[]{:S(2)}, u32[]{:S(2)}) collective-permute-start(bf16[8,128,2,128]{3,1,0,2:T(8,128)(2,1)} %bitcast.677), channel_id=1, source_target_pairs={{0,1},{1,0},{2,3},{3,2},{4,5},{5,4},{6,7},{7,6},{8,9},{9,8},{10,11... | collective-permute-start | bytes 1572872 | tf_op jit(solution)/shard_map/ppermute | solution.py:56
  91.1 5.1 %copy-start.5 = (f32[2,8,128,128]{3,0,2,1:T(2,128)}, f32[2,8,128,128]{3,0,2,1:T(2,128)S(1)}, u32[]{:S(2)}) copy-start(f32[2,8,128,128]{3,0,2,1:T(2,128)S(1)} %fusion.118) | copy-start | bytes 3145732
  92.2 95.6 %collective-permute-start.6 = (bf16[8,128,2,128]{3,1,0,2:T(8,128)(2,1)}, bf16[8,128,2,128]{3,1,0,2:T(8,128)(2,1)}, u32[]{:S(2)}, u32[]{:S(2)}) collective-permute-start(bf16[8,128,2,128]{3,1,0,2:T(8,128)(2,1)} %bitcast.675), channel_id=1, source_target_pairs={{0,1},{1,0},{2,3},{3,2},{4,5},{5,4},{6,7},{7,6},{8,9},{9,8},{10,11... | collective-permute-start | bytes 1572872 | tf_op jit(solution)/shard_map/ppermute | solution.py:56
  93.7 4.2 %copy-start.17 = (bf16[4,128,8,2,128]{4,3,2,1,0:T(2,128)(2,1)S(1)}, bf16[4,128,8,2,128]{4,3,2,1,0:T(2,128)(2,1)}, u32[]{:S(2)}) copy-start(bf16[4,128,8,2,128]{4,3,2,1,0:T(2,128)(2,1)} %get-tuple-element.25) | copy-start | bytes 6291460
  97.3 91.7 %collective-permute-start.4 = (bf16[8,128,2,128]{3,1,0,2:T(8,128)(2,1)}, bf16[8,128,2,128]{3,1,0,2:T(8,128)(2,1)}, u32[]{:S(2)}, u32[]{:S(2)}) collective-permute-start(bf16[8,128,2,128]{3,1,0,2:T(8,128)(2,1)} %bitcast.676), channel_id=1, source_target_pairs={{0,1},{1,0},{2,3},{3,2},{4,5},{5,4},{6,7},{7,6},{8,9},{9,8},{10,11... | collective-permute-start | bytes 1572872 | tf_op jit(solution)/shard_map/ppermute | solution.py:56
  117.7 74.0 %all-to-all-start.1 = ((bf16[4,128,8,2,128]{4,2,0,3,1:T(8,128)(2,1)}), bf16[4,128,8,2,128]{4,2,0,3,1:T(8,128)(2,1)}, u32[]{:S(2)}, u32[]{:S(2)}) async-start(bf16[4,128,8,2,128]{4,2,0,3,1:T(8,128)(2,1)} %copy.116), calls=%async_computation.1 | async-start | bytes 4194304 | tf_op jit(solution)/shard_map/all_to_all | solution.py:77
  129.0 9.4 %copy-start.11 = (bf16[4,8,128,2,128]{4,3,2,1,0:T(2,128)(2,1)S(1)}, bf16[4,8,128,2,128]{4,3,2,1,0:T(2,128)(2,1)}, u32[]{:S(2)}) copy-start(bf16[4,8,128,2,128]{4,3,2,1,0:T(2,128)(2,1)} %param.8) | copy-start | bytes 6291460
  138.4 51.8 %copy-start.1 = (f32[4,8,128,128]{3,2,1,0:T(8,128)}, f32[4,8,128,128]{3,2,1,0:T(8,128)S(1)}, u32[]{:S(2)}) copy-start(f32[4,8,128,128]{3,2,1,0:T(8,128)S(1)} %get-tuple-element.68) | copy-start | bytes 6291460
  138.4 4.9 %copy-start.16 = (bf16[4,128,8,2,128]{4,3,2,1,0:T(2,128)(2,1)S(1)}, bf16[4,128,8,2,128]{4,3,2,1,0:T(2,128)(2,1)}, u32[]{:S(2)}) copy-start(bf16[4,128,8,2,128]{4,3,2,1,0:T(2,128)(2,1)} %get-tuple-element.26) | copy-start | bytes 6291460
  180.0 3.4 %copy-start.21 = (f32[8,128,2,128]{3,2,1,0:T(2,128)S(1)}, f32[8,128,2,128]{3,2,1,0:T(2,128)}, u32[]{:S(2)}) copy-start(f32[8,128,2,128]{3,2,1,0:T(2,128)} %get-tuple-element.92) | copy-start | bytes 3145732
  183.4 4.5 %copy-start.6 = (f32[2,8,128,128]{3,0,2,1:T(2,128)S(1)}, f32[2,8,128,128]{3,0,2,1:T(2,128)}, u32[]{:S(2)}) copy-start(f32[2,8,128,128]{3,0,2,1:T(2,128)} %copy-done.5) | copy-start | bytes 3145732
  185.6 3.4 %copy-start.8 = (f32[2,8,128,128]{3,0,2,1:T(2,128)S(1)}, f32[2,8,128,128]{3,0,2,1:T(2,128)}, u32[]{:S(2)}) copy-start(f32[2,8,128,128]{3,0,2,1:T(2,128)} %copy-done.7) | copy-start | bytes 3145732
  191.7 11.4 %copy-start.20 = (f32[8,32,8,128]{3,2,1,0:T(8,128)S(1)}, f32[8,32,8,128]{3,2,1,0:T(8,128)}, u32[]{:S(2)}) copy-start(f32[8,32,8,128]{3,2,1,0:T(8,128)} %convert_add_fusion) | copy-start | bytes 3145732
  191.8 63.3 %all-to-all-start = ((bf16[4,128,8,2,128]{4,2,0,3,1:T(8,128)(2,1)}), bf16[4,128,8,2,128]{4,2,0,3,1:T(8,128)(2,1)}, u32[]{:S(2)}, u32[]{:S(2)}) async-start(bf16[4,128,8,2,128]{4,2,0,3,1:T(8,128)(2,1)} %copy.106), calls=%async_computation | async-start | bytes 4194304 | tf_op jit(solution)/shard_map/all_to_all | solution.py:77
  266.3 5.7 %copy-start.3 = (f32[4,8,128,128]{3,2,1,0:T(8,128)S(1)}, f32[4,8,128,128]{3,2,1,0:T(8,128)}, u32[]{:S(2)}) copy-start(f32[4,8,128,128]{3,2,1,0:T(8,128)} %copy-done.1) | copy-start | bytes 6291460
  272.7 14.8 %collective-permute-start.1 = (bf16[8,128,2,128]{3,1,0,2:T(8,128)(2,1)S(1)}, bf16[8,128,2,128]{3,1,0,2:T(8,128)(2,1)S(1)}, u32[]{:S(2)}, u32[]{:S(2)}) collective-permute-start(bf16[8,128,2,128]{3,1,0,2:T(8,128)(2,1)S(1)} %fusion.126), channel_id=1, source_target_pairs={{0,1},{1,0},{2,3},{3,2},{4,5},{5,4},{6,7},{7,6},{8,9},{9,8},{10,11... | collective-permute-start | bytes 1572872 | tf_op jit(solution)/shard_map/ppermute | solution.py:56
  274.3 24.4 %collective-permute-start.3 = (bf16[8,128,2,128]{3,1,0,2:T(8,128)(2,1)S(1)}, bf16[8,128,2,128]{3,1,0,2:T(8,128)(2,1)S(1)}, u32[]{:S(2)}, u32[]{:S(2)}) collective-permute-start(bf16[8,128,2,128]{3,1,0,2:T(8,128)(2,1)S(1)} %fusion.125), channel_id=1, source_target_pairs={{0,1},{1,0},{2,3},{3,2},{4,5},{5,4},{6,7},{7,6},{8,9},{9,8},{10,11... | collective-permute-start | bytes 1572872 | tf_op jit(solution)/shard_map/ppermute | solution.py:56
  275.0 35.0 %collective-permute-start.5 = (bf16[8,128,2,128]{3,1,0,2:T(8,128)(2,1)S(1)}, bf16[8,128,2,128]{3,1,0,2:T(8,128)(2,1)S(1)}, u32[]{:S(2)}, u32[]{:S(2)}) collective-permute-start(bf16[8,128,2,128]{3,1,0,2:T(8,128)(2,1)S(1)} %fusion.124), channel_id=1, source_target_pairs={{0,1},{1,0},{2,3},{3,2},{4,5},{5,4},{6,7},{7,6},{8,9},{9,8},{10,11... | collective-permute-start | bytes 1572872 | tf_op jit(solution)/shard_map/ppermute | solution.py:56
  276.8 43.9 %collective-permute-start.7 = (bf16[8,128,2,128]{3,1,0,2:T(8,128)(2,1)S(1)}, bf16[8,128,2,128]{3,1,0,2:T(8,128)(2,1)S(1)}, u32[]{:S(2)}, u32[]{:S(2)}) collective-permute-start(bf16[8,128,2,128]{3,1,0,2:T(8,128)(2,1)S(1)} %fusion.123), channel_id=1, source_target_pairs={{0,1},{1,0},{2,3},{3,2},{4,5},{5,4},{6,7},{7,6},{8,9},{9,8},{10,11... | collective-permute-start | bytes 1572872 | tf_op jit(solution)/shard_map/ppermute | solution.py:56
  (13 other events, 28.6 us)
